TPU v7x, 512 devices: a whole 4x8x8 slice. The times are simulated.
512 devices in a mesh: dp: 64 (over y, z_lo, core), col: 8 (over x, z_hi).
Axes of the slice: x: 4, y: 8, z: 8 (z_hi: 2, z_lo: 4; z = z_hi * 4 + z_lo), core: 2. Of those that a mesh axis runs over, the one named last changes fastest.
Arguments:
- queries: bfloat16 [16384, 4096], P('dp'), as said below
- passages: bfloat16 [8, 256, 4096], P('col', 'dp'), as said below
- teacher: float32 [16384, 2048], P('dp', 'col'), as said below
Outputs:
- mean_loss: float32 [], replicated
- query_grads: bfloat16 [16384, 4096], P('dp')
- passage_grads: float32 [8, 256, 4096], P('col', 'dp')
Inputs may be any that keep to these rules, and one draw needn't show every extreme that they name: `queries`: query entries of order one over the square root of 4096. `passages`: passage entries of order one over the square root of 4096. `teacher`: reranker scores.
All inputs are finite; a program needn't handle non-finite values.
Results may differ from a plain program's by a relative error of at most 0.017.
Values may be sent and summed in bfloat16 or wider, within the bound.
A program may use at most 64 MiB of HBM per device.

v0:
```python
import jax
import jax.numpy as jnp
from jax import lax
from jax.sharding import PartitionSpec as P

INV_TEMP = 50.0
CONTRACT_LAST = (((1,), (1,)), ((), ()))
CONTRACT_FIRST = (((0,), (0,)), ((), ()))


def on_device(queries, passages, teacher):
    own_rows = passages[0]
    query_count = queries.shape[0]
    column_count = teacher.shape[1]
    cycle_size = lax.axis_size("dp")
    cycle_index = lax.axis_index("dp")
    gathered = lax.all_gather(own_rows, "dp", axis=0, tiled=True)
    student = (
        lax.dot_general(queries, gathered, CONTRACT_LAST, preferred_element_type=jnp.float32)
        * INV_TEMP
    )
    row_peaks = lax.pmax((jnp.max(teacher, axis=1), jnp.max(student, axis=1)), "col")
    column_peaks = lax.pmax((jnp.max(teacher, axis=0), jnp.max(student, axis=0)), "dp")
    row_sums = lax.psum(
        (
            jnp.sum(jnp.exp(teacher - row_peaks[0][:, None]), axis=1),
            jnp.sum(jnp.exp(student - row_peaks[1][:, None]), axis=1),
        ),
        "col",
    )
    column_sums = lax.psum(
        (
            jnp.sum(jnp.exp(teacher - column_peaks[0][None, :]), axis=0),
            jnp.sum(jnp.exp(student - column_peaks[1][None, :]), axis=0),
        ),
        "dp",
    )
    row_teacher = row_peaks[0] + jnp.log(row_sums[0])
    row_student = row_peaks[1] + jnp.log(row_sums[1])
    col_teacher = column_peaks[0] + jnp.log(column_sums[0])
    col_student = column_peaks[1] + jnp.log(column_sums[1])
    row_target = jnp.exp(teacher - row_teacher[:, None])
    row_model = jnp.exp(student - row_student[:, None])
    col_target = jnp.exp(teacher - col_teacher[None, :])
    col_model = jnp.exp(student - col_student[None, :])
    col_side = jnp.where(lax.axis_index("col") == 0, 1.0, 0.0).astype(jnp.float32)
    cycle_side = jnp.where(cycle_index == 0, 1.0, 0.0).astype(jnp.float32)
    divergence = (
        jnp.sum((row_target + col_target) * (teacher - student))
        + col_side * jnp.sum(row_student - row_teacher)
        + cycle_side * jnp.sum(col_student - col_teacher)
    )
    divergence_sum = lax.psum(divergence, ("dp", "col"))
    mean_loss = divergence_sum / (query_count * cycle_size + column_count * lax.axis_size("col"))
    gradient = (row_model - row_target + (col_model - col_target)).astype(jnp.bfloat16)
    partial_sum = jnp.dot(gradient, gathered, preferred_element_type=jnp.float32) * INV_TEMP
    query_grads = lax.psum(partial_sum.astype(jnp.bfloat16), "col")
    passage_grads = lax.psum_scatter(
        lax.dot_general(gradient, queries, CONTRACT_FIRST, preferred_element_type=jnp.float32)
        * INV_TEMP,
        "dp",
        scatter_dimension=0,
        tiled=True,
    )
    return (mean_loss, query_grads, passage_grads[None])


def solution(mesh):
    return jax.shard_map(
        on_device,
        mesh=mesh,
        in_specs=(P("dp", None), P("col", "dp", None), P("dp", "col")),
        out_specs=(P(), P("dp", None), P("col", "dp", None)),
        check_vma=False,
    )
```

profile of v0, /device:TPU:1, one launch (start us, length us, event | category | flops | bytes accessed | tf_op | source)
XLA Modules:
  0.0 1392.9 jit_solution(8243985038314645196)
XLA Ops:
  7.2 0.0 copy-start
  7.2 0.0 all-gather.3.cloned.1.call-start
  7.2 1.6 copy.7
  8.8 0.0 all-gather.3.cloned.1.call-update
  8.8 0.0 all-reduce.8.cloned.1.call-start
  8.9 1.1 reduce_max.36
  9.9 0.0 copy-start.1
  10.0 127.2 %all-gather.3.cloned.1.call-done = bf16[1,256,4096]{2,0,1:T(2,128)(2,1)} async-done(((bf16[1,4,4096]{2,0,1:T(2,128)(2,1)}), bf16[1,256,4096]{2,0,1:T(2,128)(2,1)}) %all-gather.3.cloned.1.call-update) | async-done | bytes 2097168 | tf_op jit(solution)/shard_map/all_gather | solution.py:17
  137.2 0.0 copy-done
  137.2 4.9 fusion.9
  142.1 26.3 %all-reduce.2 = (f32[256]{0:T(256)S(1)}, f32[256]{0:T(256)S(1)}) all-reduce(f32[256]{0:T(256)S(1)} %reduce_max.36, f32[256]{0:T(256)S(1)} %get-tuple-element.7), channel_id=1, replica_groups=mesh['dp'=64,'col'=8] {'col'}, use_global_device_ids=true, to_apply=%region_1.0 | all-reduce | flops 512 | bytes 4096 | tf_op jit(solution)/shard_map/pmax | solution.py:22
  168.4 0.0 copy-done.1
  168.4 0.2 exponential_reduce_fusion.3
  168.6 136.9 %all-reduce.1 = (f32[256]{0:T(256)S(1)}, f32[256]{0:T(256)S(1)}) all-reduce(f32[256]{0:T(256)S(1)} %get-tuple-element.6, f32[256]{0:T(256)S(1)} %get-tuple-element.9), channel_id=1, replica_groups=mesh['dp'=64,'col'=8] {'dp'}, use_global_device_ids=true, to_apply=%region_15.0 | all-reduce | flops 512 | bytes 4096 | tf_op jit(solution)/shard_map/pmax | solution.py:23
  305.4 0.1 exponential_reduce_fusion.2
  305.5 133.4 %psum.43 = f32[256]{0:T(256)S(1)} all-reduce(f32[256]{0:T(256)S(1)} %exponential_reduce_fusion.2), channel_id=1, replica_groups=mesh['dp'=64,'col'=8] {'dp'}, use_global_device_ids=true, to_apply=%region_7.0 | all-reduce | flops 256 | bytes 2048 | tf_op jit(solution)/shard_map/psum | solution.py:31
  438.9 20.4 %psum.42 = f32[256]{0:T(256)S(1)} all-reduce(f32[256]{0:T(256)S(1)} %get-tuple-element.8), channel_id=1, replica_groups=mesh['dp'=64,'col'=8] {'col'}, use_global_device_ids=true, to_apply=%region_3.0 | all-reduce | flops 256 | bytes 2048 | tf_op jit(solution)/shard_map/psum | solution.py:24
  459.3 0.8 exponential_reduce_fusion
  460.1 25.9 %psum.44 = f32[256]{0:T(256)S(1)} all-reduce(f32[256]{0:T(256)S(1)} %get-tuple-element.4), channel_id=1, replica_groups=mesh['dp'=64,'col'=8] {'col'}, use_global_device_ids=true, to_apply=%region_12.0 | all-reduce | flops 256 | bytes 2048 | tf_op jit(solution)/shard_map/psum | solution.py:24
  486.1 0.6 subtract_reduce_fusion.1
  486.7 140.8 %psum.45 = f32[256]{0:T(256)S(1)} all-reduce(f32[256]{0:T(256)S(1)} %get-tuple-element.3), channel_id=1, replica_groups=mesh['dp'=64,'col'=8] {'dp'}, use_global_device_ids=true, to_apply=%region_17.18 | all-reduce | flops 256 | bytes 2048 | tf_op jit(solution)/shard_map/psum | solution.py:31
  627.4 0.6 subtract_reduce_fusion
  628.1 0.2 add_convert_fusion
  628.2 2.7 convolution_multiply_fusion
  631.0 0.0 all-reduce.8.cloned.1.call-update
  631.0 0.0 all-reduce.6.cloned.1.call-start
  631.0 6.2 fusion
  637.2 0.0 all-reduce.6.cloned.1.call-update
  637.3 1.3 dynamic-slice
  641.2 95.0 %psum.46 = f32[]{:T(128)} all-reduce(f32[]{:T(128)S(6)} %add.44), channel_id=1, replica_groups=mesh['dp'=64,'col'=8] {'dp','col'}, use_global_device_ids=true, to_apply=%region_19.20 | all-reduce | flops 1 | bytes 8 | tf_op jit(solution)/shard_map/psum | solution.py:53
  736.9 438.2 %all-reduce.8.cloned.1.call-done = f32[256,4096]{1,0:T(8,128)} async-done(((f32[256,4096]{1,0:T(8,128)}), f32[256,4096]{1,0:T(8,128)}) %all-reduce.8.cloned.1.call-update) | async-done | bytes 4194320
  1175.1 1.5 dynamic-slice_bitcast_fusion
  1176.7 205.5 %all-reduce.6.cloned.1.call-done = bf16[256,4096]{1,0:T(8,128)(2,1)} async-done(((bf16[256,4096]{1,0:T(8,128)(2,1)}), bf16[256,4096]{1,0:T(8,128)(2,1)}) %all-reduce.6.cloned.1.call-update) | async-done | bytes 2097168 | tf_op jit(solution)/shard_map/psum | solution.py:57
  1382.1 3.1 copy.21
  (2 shorter events, 0.0 us)
Async XLA Ops:
  7.2 130.0 %copy-start = (bf16[256,4096]{1,0:T(8,128)(2,1)S(1)}, bf16[256,4096]{1,0:T(8,128)(2,1)}, u32[]{:S(2)}) copy-start(bf16[256,4096]{1,0:T(8,128)(2,1)} %param.3) | copy-start | bytes 6291460
  7.2 130.0 %all-gather.3.cloned.1.call-start = ((), (), s32[]{:S(2)}) async-start(), calls=%async_computation.1 | async-start | bytes 4259840 | tf_op jit(solution)/shard_map/all_gather | solution.py:17
  8.8 1166.3 %all-reduce.8.cloned.1.call-start = ((), (), s32[]{:S(2)}) async-start(), calls=%async_computation.2 | async-start | bytes 8388608
  9.9 158.4 %copy-start.1 = (f32[256,256]{1,0:T(8,128)S(1)}, f32[256,256]{1,0:T(8,128)}, u32[]{:S(2)}) copy-start(f32[256,256]{1,0:T(8,128)} %param.5) | copy-start | bytes 786436
  631.0 751.1 %all-reduce.6.cloned.1.call-start = ((), (), s32[]{:S(2)}) async-start(), calls=%async_computation | async-start | bytes 4194304 | tf_op jit(solution)/shard_map/psum | solution.py:57
Sparse Core Ops, SparseCore 0:
  10.7 126.4 all-gather.2
  631.1 543.9 all-reduce.7
  1178.9 203.1 all-reduce.5
where the time goes:
time: 1390 us
  waiting for transfers between devices  771 us (55%)
  blocking collectives  579 us (42%)
  between operations  18.1 us (1%)
    unnamed x4, waiting for transfers between devices  438 us
    psum x2, blocking collectives, on_device(): lax.psum((jnp.sum(jnp.exp(teacher - column_peaks[0][None, :]), axis=0), j...  274 us
    psum x1, waiting for transfers between devices, on_device(): query_grads = lax.psum(partial_sum.astype(jnp.bfloat16), 'col')  205 us
    pmax x1, blocking collectives, on_device(): lax.pmax((jnp.max(teacher, axis=0), jnp.max(student, axis=0)), 'dp')  137 us
    all_gather x1, waiting for transfers between devices, on_device(): gathered = lax.all_gather(own_rows, 'dp', axis=0, tiled=True)  127 us
    psum x1, blocking collectives, on_device(): divergence_sum = lax.psum(divergence, ('dp', 'col'))  95 us
    psum x2, blocking collectives, on_device(): lax.psum((jnp.sum(jnp.exp(teacher - row_peaks[0][:, None]), axis=1), jnp....  46.3 us
  transfers between devices with their start and end apart: 3, of which 3 were waited for; matrix products, arithmetic and copies ran while one was open for 1% of the time, Pallas kernels for 0%

commit v1 on v0

v1 whole, which is shorter than its diff:
```python
import functools

import jax
import jax.numpy as jnp
from jax import lax
from jax.experimental import pallas as pl
from jax.experimental.pallas import tpu as pltpu
from jax.sharding import PartitionSpec as P

INV_TEMP = 50.0
MESH = pl.DeviceIdType.MESH
F32 = jnp.float32
BF16 = jnp.bfloat16
NT = (((1,), (1,)), ((), ()))
NN = (((1,), (0,)), ((), ()))


class Links:
    def __init__(self):
        self.sent = []

    def send(self, src, dst, send_sem, recv_sem, device):
        copy = pltpu.make_async_remote_copy(
            src_ref=src, dst_ref=dst, send_sem=send_sem, recv_sem=recv_sem, device_id=device, device_id_type=MESH
        )
        copy.start()
        self.sent.append(copy)

    def arrive(self, ref, send_sem, recv_sem, device):
        pltpu.make_async_remote_copy(
            src_ref=ref, dst_ref=ref, send_sem=send_sem, recv_sem=recv_sem, device_id=device, device_id_type=MESH
        ).wait_recv()

    def drain(self):
        for copy in self.sent:
            copy.wait_send()
        self.sent = []


def kernel(
    q_ref, p_ref, t_ref,
    loss_ref, qg_ref, pg_ref,
    swap, stage, pa, xsrc, xgot, xstage, pb1, pb2, qh, pn, pall,
    student, sgot, colz, coly, rowx, lossb,
    grads, gt, pgf, rs_out, rs_in, rs2_out, rs2_in, fin, outb,
    q_sem, swap_s, swap_r, paz_s, paz_r, pay_s, pay_r, x_s, x_r,
    b1_s, b1_r, b2_s, b2_r, ring1_s, ring1_r, ring2_s, ring2_r,
    st_s, st_r, cz_s, cz_r, cy_s, cy_r, rx_s, rx_r, lo_s, lo_r,
    g_s, g_r, ry_s, ry_r, rz_s, rz_r, f_s, f_r, o_s, o_r, own_sem,
):
    dp = lax.axis_index("dp")
    col = lax.axis_index("col")
    core = lax.rem(dp, 2)
    zl = lax.rem(dp // 2, 4)
    y = dp // 8
    x = col // 2
    zh = lax.rem(col, 2)
    z = zh * 4 + zl
    par = lax.rem(x, 2)
    other = 1 - core
    links = Links()

    def at(xx, yy, zz, cc):
        xx, yy, zz = lax.rem(xx + 4, 4), lax.rem(yy + 8, 8), lax.rem(zz + 8, 8)
        return ((yy * 4 + lax.rem(zz, 4)) * 2 + cc, xx * 2 + zz // 4)

    sib = at(x, y, z, other)

    def y_peer(i):
        return at(x, i, z, core)

    def z_peer(i):
        return at(x, y, i, core)

    def zl_peer(i):
        return at(x, y, zh * 4 + i, core)

    def zc_peer(i):
        return at(x, y, zh * 4 + i // 2, lax.rem(i, 2))

    def col_peer(i):
        return (dp, i)

    def x_peer(i):
        return at(i, y, z, core)

    zc = zl * 2 + core

    peers = [y_peer(y + d) for d in range(1, 8)]
    peers += [zc_peer(lax.rem(zc + d, 8)) for d in range(1, 8)]
    peers += [col_peer(lax.rem(col + d, 8)) for d in range(1, 8)]
    peers += [at(x, y, (1 - zh) * 4 + lax.rem(zl + d, 4), core) for d in range(1, 4)]
    peers += [at(x + 1, y, z, other), at(x - 1, y, z, other)]
    barrier = pltpu.get_barrier_semaphore()
    for device in peers:
        pl.semaphore_signal(barrier, inc=1, device_id=device, device_id_type=MESH)
    pl.semaphore_wait(barrier, len(peers))

    links.send(p_ref.at[other], swap, swap_s, swap_r, sib)
    mine = pl.ds(pl.multiple_of(core * 256, 256), 256)
    theirs = pl.ds(pl.multiple_of(other * 256, 256), 256)
    half = pl.ds(pl.multiple_of(core * 2048, 2048), 2048)
    other_half = pl.ds(pl.multiple_of(other * 2048, 2048), 2048)
    own_q = pltpu.make_async_copy(q_ref.at[:, half], qh.at[mine], own_sem)
    own_q.start()
    links.send(q_ref.at[:, other_half], qh.at[mine], q_sem.at[0], q_sem.at[1], sib)

    links.arrive(swap, swap_s, swap_r, sib)
    a = p_ref[core].astype(F32)
    b = swap[...].astype(F32)
    first = jnp.where(core == 0, a, b)
    second = jnp.where(core == 0, b, a)
    for src, block in enumerate((first, second)):
        for k in range(4):
            row = 8 * (k // 2) + 4 * src
            stage[row : row + 4, 512 * (k % 2) : 512 * (k % 2) + 512] = block[4 * k : 4 * k + 4]
    share = stage[...]
    pa[y, zl] = share.astype(BF16)
    for p in range(2):
        rows = share[8 * p : 8 * p + 8]
        xsrc[p] = jnp.concatenate([rows[:, :512], rows[:, 512:]], axis=0).astype(BF16)

    for d in range(1, 4):
        to = lax.rem(zl + d, 4)
        links.send(pa.at[y, zl], pa.at[y, zl], paz_s.at[d - 1], paz_r.at[zl], zl_peer(to))
    for d in range(1, 4):
        to = lax.rem(x + d, 4)
        links.send(xsrc.at[lax.rem(to, 2)], xgot.at[x], x_s.at[d - 1], x_r.at[x], x_peer(to))

    def reduce_rows(values):
        top = jnp.max(values, axis=1, keepdims=True)
        return top, jnp.sum(jnp.exp(values - top), axis=1, keepdims=True)

    def reduce_cols(values):
        top = jnp.max(values, axis=0, keepdims=True)
        return top, jnp.sum(jnp.exp(values - top), axis=0, keepdims=True)

    zeros6 = jnp.zeros((6, 256), F32)
    lane = lax.broadcasted_iota(jnp.int32, (256, 128), 1)

    def combine(slots):
        tops = slots[:, 0, :]
        top = jnp.max(tops, axis=0, keepdims=True)
        return top, jnp.sum(jnp.exp(tops - top) * slots[:, 1, :], axis=0, keepdims=True)

    def send_stats(kind, values):
        top, total = reduce_cols(values)
        colz[kind, zc] = jnp.concatenate([top, total, zeros6], axis=0)
        for d in range(1, 8):
            links.send(colz.at[kind, zc], colz.at[kind, zc], cz_s.at[kind, d - 1], cz_r.at[kind, zc],
                       zc_peer(lax.rem(zc + d, 8)))
        top, total = reduce_rows(values)
        packed = jnp.where(lane == 0, top, jnp.where(lane == 1, total, 0.0))
        rowx[kind, col] = packed.T[:8]
        for d in range(1, 8):
            links.send(rowx.at[kind, col], rowx.at[kind, col], rx_s.at[kind, d - 1], rx_r.at[kind, col],
                       col_peer(lax.rem(col + d, 8)))

    def pass_stats(kind):
        for d in range(1, 8):
            i = lax.rem(zc + d, 8)
            links.arrive(colz.at[kind, i], cz_s.at[kind, d - 1], cz_r.at[kind, i], zc_peer(i))
        top, total = combine(colz[kind])
        coly[kind, y] = jnp.concatenate([top, total, zeros6], axis=0)
        for d in range(1, 8):
            links.send(coly.at[kind, y], coly.at[kind, y], cy_s.at[kind, d - 1], cy_r.at[kind, y], y_peer(y + d))

    def finish_stats(kind):
        for d in range(1, 8):
            i = lax.rem(col + d, 8)
            links.arrive(rowx.at[kind, i], rx_s.at[kind, d - 1], rx_r.at[kind, i], col_peer(i))
        top, total = combine(rowx[kind])
        row_log = top + jnp.log(total)
        for d in range(1, 8):
            i = lax.rem(y + d, 8)
            links.arrive(coly.at[kind, i], cy_s.at[kind, d - 1], cy_r.at[kind, i], y_peer(i))
        top, total = combine(coly[kind])
        return row_log, top + jnp.log(total)

    def ring(me, view, device, send_sem, recv_sem):
        for step in range(1, 5):
            for way, sign in enumerate((1, -1)):
                block = lax.rem(me - sign * (step - 1) + 8, 8)
                for c in range(2):
                    if step > 1:
                        links.arrive(view(block, c), send_sem.at[way, step - 2, c], recv_sem.at[way, step - 2, c],
                                     device(me - sign))
                    if step == 4 and c != way:
                        continue
                    links.send(view(block, c), view(block, c), send_sem.at[way, step - 1, c],
                               recv_sem.at[way, step - 1, c], device(me + sign))
            yield
        block = lax.rem(me + 4, 8)
        for way, sign in enumerate((1, -1)):
            links.arrive(view(block, way), send_sem.at[way, 3, way], recv_sem.at[way, 3, way], device(me - sign))
        yield

    teacher = t_ref[...]
    send_stats(0, teacher)

    xgot[x] = xsrc[par]
    for d in range(1, 4):
        i = lax.rem(x + d, 4)
        links.arrive(xgot.at[i], x_s.at[d - 1], x_r.at[i], x_peer(i))
    for i in range(4):
        both = xgot[i].astype(F32)
        xstage[8 * i : 8 * i + 8, :512] = both[:8]
        xstage[8 * i : 8 * i + 8, 512:] = both[8:]
    pb1[y, z] = xstage[:, :512].astype(BF16)
    pb2[z, y] = xstage[:, 512:].astype(BF16)

    for d in range(1, 4):
        i = lax.rem(zl + d, 4)
        links.arrive(pa.at[y, i], paz_s.at[d - 1], paz_r.at[i], zl_peer(i))
    own_ring = ring(y, lambda b, c: pa.at[b, pl.ds(2 * c, 2)], y_peer, pay_s, pay_r)
    next(own_ring)
    for d in range(1, 8):
        i = lax.rem(z + d, 8)
        links.send(pb1.at[y, z], pb1.at[y, z], b1_s.at[d - 1], b1_r.at[z], z_peer(i))
    pass_stats(0)
    next(own_ring)
    next(own_ring)
    for d in range(1, 8):
        i = lax.rem(y + d, 8)
        links.send(pb2.at[z, y], pb2.at[z, y], b2_s.at[d - 1], b2_r.at[y], y_peer(i))
    next(own_ring)
    row_teacher, col_teacher = finish_stats(0)
    next(own_ring)

    @pl.loop(0, 16)
    def _(pair):
        yy, zz = pair // 2, lax.rem(pair, 2) * 2
        b0 = pa[yy, zz].astype(F32)
        b1 = pa[yy, zz + 1].astype(F32)
        rows = pl.ds(pl.multiple_of(pair * 16, 16), 16)
        for k in range(2):
            both = jnp.concatenate([b0[8 * k : 8 * k + 8], b1[8 * k : 8 * k + 8]], axis=0)
            pn[rows, 1024 * k : 1024 * k + 1024] = both.astype(BF16)

    own_q.wait()
    links.arrive(qh.at[theirs], q_sem.at[0], q_sem.at[1], sib)
    student[1] = lax.dot_general(qh[theirs], pn[...], NT, preferred_element_type=F32)
    links.send(student.at[1], sgot, st_s, st_r, sib)
    own_part = lax.dot_general(qh[mine], pn[...], NT, preferred_element_type=F32)

    for d in range(1, 8):
        i = lax.rem(z + d, 8)
        links.arrive(pb1.at[y, i], b1_s.at[d - 1], b1_r.at[i], z_peer(i))
    ring1 = ring(y, lambda b, c: pb1.at[b, pl.ds(4 * c, 4)], y_peer, ring1_s, ring1_r)
    next(ring1)

    links.arrive(sgot, st_s, st_r, sib)
    scores = (own_part + sgot[...]) * INV_TEMP
    student[0] = scores
    send_stats(1, scores)
    pass_stats(1)
    for d in range(1, 8):
        i = lax.rem(y + d, 8)
        links.arrive(pb2.at[z, i], b2_s.at[d - 1], b2_r.at[i], y_peer(i))
    ring2 = ring(z, lambda b, c: pb2.at[b, pl.ds(4 * c, 4)], z_peer, ring2_s, ring2_r)
    next(ring2)
    row_student, col_student = finish_stats(1)

    def down(row):
        return jnp.broadcast_to(row, (128, 256)).T[:, :1]

    scores = student[0]
    teacher = t_ref[...]
    row_target = jnp.exp(teacher - down(row_teacher))
    col_target = jnp.exp(teacher - col_teacher)
    gradient = (jnp.exp(scores - down(row_student)) - row_target) + (jnp.exp(scores - col_student) - col_target)
    grads[x, zh, core] = gradient.astype(BF16)

    own_grads = grads.at[x, zh, core]
    links.send(own_grads, own_grads, g_s.at[0], g_r.at[x, zh, core], sib)
    links.send(own_grads, own_grads, g_s.at[1], g_r.at[x, zh, core], at(x, y, z + 4, core))
    for d in range(1, 4):
        links.send(own_grads, own_grads, g_s.at[1 + d], g_r.at[x, zh, core], x_peer(x + d))

    terms = (row_target + col_target) * (teacher - scores)
    terms = jnp.sum(terms.reshape(32, 8, 256), axis=0)
    once = jnp.where(col == 0, 1.0, 0.0) * (row_student - row_teacher)
    once += jnp.where(dp == 0, 1.0, 0.0) * (col_student - col_teacher)
    terms += jnp.concatenate([once, jnp.zeros((7, 256), F32)], axis=0)
    terms = terms[:, :128] + terms[:, 128:]

    def send_loss(level, me, peer, value):
        lossb[level, me] = value
        for d in range(1, 8):
            links.send(lossb.at[level, me], lossb.at[level, me], lo_s.at[level, d - 1], lo_r.at[level, me],
                       peer(lax.rem(me + d, 8)))

    def sum_loss(level, me, peer):
        for d in range(1, 8):
            i = lax.rem(me + d, 8)
            links.arrive(lossb.at[level, i], lo_s.at[level, d - 1], lo_r.at[level, i], peer(i))
        return jnp.sum(lossb[level], axis=0)

    send_loss(0, col, col_peer, terms)

    links.arrive(grads.at[x, zh, other], g_s.at[0], g_r.at[x, zh, other], sib)
    for c in range(2):
        gt[:, 256 * c : 256 * c + 256] = grads[x, zh, c].astype(F32).T.astype(BF16)
    for k in range(4):
        lanes = slice(512 * k, 512 * k + 512)
        pgf[:, lanes] = lax.dot_general(gt[...], qh[:, lanes], NN, preferred_element_type=F32) * INV_TEMP

    @pl.loop(0, 32)
    def _(chip):
        rows = pl.ds(pl.multiple_of(chip * 8, 8), 8)
        both = jnp.concatenate([pgf[rows, :1024], pgf[rows, 1024:]], axis=0)
        rs_out[chip // 4, lax.rem(chip, 4)] = both.astype(BF16)

    for d in range(1, 8):
        i = lax.rem(y + d, 8)
        links.send(rs_out.at[i], rs_in.at[y], ry_s.at[d - 1], ry_r.at[y], y_peer(i))

    partner = grads.at[x, 1 - zh, core]
    links.arrive(partner, g_s.at[1], g_r.at[x, 1 - zh, core], at(x, y, z + 4, core))
    for d in range(1, 4):
        links.send(partner, partner, g_s.at[4 + d], g_r.at[x, 1 - zh, core], x_peer(x + d))
    links.send(partner, partner, g_s.at[8], g_r.at[x, 1 - zh, core], sib)
    next(ring1)
    next(ring2)
    send_loss(1, zc, zc_peer, sum_loss(0, col, col_peer))
    for d in range(1, 4):
        i = lax.rem(x + d, 4)
        block = grads.at[i, zh, core]
        links.arrive(block, g_s.at[1 + d], g_r.at[i, zh, core], x_peer(i))
        links.send(block, block, g_s.at[8 + d], g_r.at[i, zh, core], sib)
    next(ring1)
    next(ring2)
    send_loss(2, y, y_peer, sum_loss(1, zc, zc_peer))
    for d in range(1, 4):
        i = lax.rem(x + d, 4)
        block = grads.at[i, 1 - zh, core]
        links.arrive(block, g_s.at[4 + d], g_r.at[i, 1 - zh, core], x_peer(i))
        links.send(block, block, g_s.at[11 + d], g_r.at[i, 1 - zh, core], sib)
    next(ring1)
    next(ring2)

    total = None
    for d in range(1, 8):
        i = lax.rem(y + d, 8)
        links.arrive(rs_in.at[i], ry_s.at[d - 1], ry_r.at[i], y_peer(i))
    rs_in[y] = rs_out[y]
    for i in range(4):
        total = rs_in[0, i].astype(F32)
        for j in range(1, 8):
            total += rs_in[j, i].astype(F32)
        rs2_out[i] = total.astype(BF16)
    for d in range(1, 4):
        i = lax.rem(zl + d, 4)
        links.send(rs2_out.at[i], rs2_in.at[zl], rz_s.at[d - 1], rz_r.at[zl], zl_peer(i))
    rs2_in[zl] = rs2_out[zl]
    next(ring1)
    next(ring2)

    @pl.loop(0, 32)
    def _(pair):
        group, yy, zz = pair // 16, lax.rem(pair // 2, 8), lax.rem(pair, 2) * 2
        rows = pl.ds(pl.multiple_of(lax.rem(pair, 16) * 16, 16), 16)
        for part in range(2):
            zf = group * 4 + zz
            if part == 0:
                b0, b1 = pb1[yy, zf].astype(F32), pb1[yy, zf + 1].astype(F32)
            else:
                b0, b1 = pb2[zf, yy].astype(F32), pb2[zf + 1, yy].astype(F32)
            for i in range(4):
                both = jnp.concatenate([b0[8 * i : 8 * i + 8], b1[8 * i : 8 * i + 8]], axis=0)
                pall[i, group, rows, 512 * part : 512 * part + 512] = both.astype(BF16)

    for i in range(3):
        j = lax.rem(zl + i + 1, 4)
        links.arrive(rs2_in.at[j], rz_s.at[i], rz_r.at[j], zl_peer(j))
    total = rs2_in[0].astype(F32)
    for j in range(1, 4):
        total += rs2_in[j].astype(F32)
    for c in range(2):
        piece = jnp.concatenate([total[4 * c : 4 * c + 4], total[8 + 4 * c : 12 + 4 * c]], axis=0)
        stage[8 * c : 8 * c + 8] = piece
    fin[core] = stage[pl.ds(pl.multiple_of(core * 8, 8), 8)]
    links.send(stage.at[pl.ds(pl.multiple_of(other * 8, 8), 8)], fin.at[core], f_s, f_r, sib)

    for i in range(4):
        for h in range(2):
            i_dyn = lax.rem(x + i, 4)
            h_dyn = lax.rem(zh + h, 2)
            if i == 0 and h == 0:
                continue
            links.arrive(grads.at[i_dyn, h_dyn, other], g_s.at[0], g_r.at[i_dyn, h_dyn, other], sib)

    lanes = pl.ds(pl.multiple_of(core * 2048 + par * 1024, 1024), 1024)
    for c in range(2):
        cc = jnp.where(core == c, 1, 0)
        del cc
        for part in range(2):
            sl = slice(512 * part, 512 * part + 512)
            acc = jnp.zeros((256, 512), F32)
            for i in range(4):
                for h in range(2):
                    acc += lax.dot_general(grads[i, h, c], pall[i, h, :, sl], NN, preferred_element_type=F32)
            outb[c, :, sl] = (acc * INV_TEMP).astype(BF16)
        for way in range(2):
            rows = pl.ds(128 * way, 128)
            links.send(outb.at[c, rows], qg_ref.at[rows, lanes], o_s.at[c, way], o_r.at[core, way],
                       at(x + 1 - 2 * way, y, z, c))
    links.send(outb.at[other], qg_ref.at[:, lanes], o_s.at[0, 2], o_r.at[core, 2], sib)
    own_out = pltpu.make_async_copy(outb.at[core], qg_ref.at[:, lanes], own_sem)
    own_out.start()

    loss_ref[0, 0] = jnp.sum(sum_loss(2, y, y_peer)) / (256 * 64 + 256 * 8)
    links.arrive(fin.at[other], f_s, f_r, sib)
    for h in range(2):
        for k in range(2):
            start = 2048 * h + 1024 * k
            pg_ref[:, start : start + 1024] = fin[h, 4 * k : 4 * k + 4]

    far = pl.ds(pl.multiple_of(other * 2048 + par * 1024, 1024), 1024)
    links.arrive(qg_ref.at[:, far], o_s.at[0, 2], o_r.at[other, 2], sib)
    for c in range(2):
        lanes = pl.ds(pl.multiple_of(c * 2048 + (1 - par) * 1024, 1024), 1024)
        for way in range(2):
            links.arrive(qg_ref.at[pl.ds(128 * way, 128), lanes], o_s.at[c, way], o_r.at[c, way],
                         at(x - 1 + 2 * way, y, z, c))
    own_out.wait()
    links.drain()


def on_device(queries, passages, teacher):
    pieces = passages[0].reshape(4, 2, 4, 512).transpose(1, 2, 0, 3).reshape(2, 16, 512)
    dma = pltpu.SemaphoreType.DMA
    vmem = pltpu.VMEM
    loss, query_grads, passage_grads = pl.pallas_call(
        kernel,
        out_shape=(
            jax.ShapeDtypeStruct((1, 1), F32),
            jax.ShapeDtypeStruct((256, 4096), BF16),
            jax.ShapeDtypeStruct((4, 4096), F32),
        ),
        in_specs=[
            pl.BlockSpec(memory_space=pl.ANY),
            pl.BlockSpec(memory_space=pltpu.VMEM),
            pl.BlockSpec(memory_space=pltpu.VMEM),
        ],
        out_specs=(
            pl.BlockSpec(memory_space=pltpu.SMEM),
            pl.BlockSpec(memory_space=pl.ANY),
            pl.BlockSpec(memory_space=pltpu.VMEM),
        ),
        scratch_shapes=[
            vmem((16, 512), BF16),
            vmem((16, 1024), F32),
            vmem((8, 4, 16, 1024), BF16),
            vmem((2, 16, 512), BF16),
            vmem((4, 16, 512), BF16),
            vmem((32, 1024), F32),
            vmem((8, 8, 32, 512), BF16),
            vmem((8, 8, 32, 512), BF16),
            vmem((512, 2048), BF16),
            vmem((256, 2048), BF16),
            vmem((4, 2, 256, 1024), BF16),
            vmem((2, 256, 256), F32),
            vmem((256, 256), F32),
            vmem((2, 8, 8, 256), F32),
            vmem((2, 8, 8, 256), F32),
            vmem((2, 8, 8, 256), F32),
            vmem((3, 8, 8, 128), F32),
            vmem((4, 2, 2, 256, 256), BF16),
            vmem((256, 512), BF16),
            vmem((256, 2048), F32),
            vmem((8, 4, 16, 1024), BF16),
            vmem((8, 4, 16, 1024), BF16),
            vmem((4, 16, 1024), BF16),
            vmem((4, 16, 1024), BF16),
            vmem((2, 8, 1024), F32),
            vmem((2, 256, 1024), BF16),
            dma((2,)),
            dma, dma,
            dma((3,)), dma((4,)),
            dma((2, 4, 2)), dma((2, 4, 2)),
            dma((3,)), dma((4,)),
            dma((7,)), dma((8,)),
            dma((7,)), dma((8,)),
            dma((2, 4, 2)), dma((2, 4, 2)),
            dma((2, 4, 2)), dma((2, 4, 2)),
            dma, dma,
            dma((2, 7)), dma((2, 8)),
            dma((2, 7)), dma((2, 8)),
            dma((2, 7)), dma((2, 8)),
            dma((3, 7)), dma((3, 8)),
            dma((15,)), dma((4, 2, 2)),
            dma((7,)), dma((8,)),
            dma((3,)), dma((4,)),
            dma, dma,
            dma((2, 3)), dma((2, 3)),
            dma,
        ],
        compiler_params=pltpu.CompilerParams(
            collective_id=0, has_side_effects=True, vmem_limit_bytes=48 * 2**20
        ),
    )(queries, pieces, teacher)
    return loss[0, 0], query_grads, passage_grads[None]


def solution(mesh):
    return jax.shard_map(
        on_device,
        mesh=mesh,
        in_specs=(P("dp", None), P("col", "dp", None), P("dp", "col")),
        out_specs=(P(), P("dp", None), P("col", "dp", None)),
        check_vma=False,
    )
```

time: 1390 us -> 131 us (0.09)
  waiting for transfers between devices: 771 us -> 0 us
  blocking collectives: 579 us -> 0 us
  Pallas kernels: 0 us -> 123 us
  between operations: 18.1 us -> 2.41 us
    unnamed x4 -> x0, waiting for transfers between devices: 438 us -> none
    psum x5 -> x0, blocking collectives: 416 us -> none  [the longest x2 274 us: on_device(): lax.psum((jnp.sum(jnp.exp(teacher - column_peaks[0][None, :]), axis=0), j...]
    psum x1 -> x0, waiting for transfers between devices: 205 us -> none  [on_device(): query_grads = lax.psum(partial_sum.astype(jnp.bfloat16), 'col')]
    pmax x2 -> x0, blocking collectives: 163 us -> none  [the longest x1 137 us: on_device(): lax.pmax((jnp.max(teacher, axis=0), jnp.max(student, axis=0)), 'dp')]
    all_gather x1 -> x0, waiting for transfers between devices: 127 us -> none  [on_device(): gathered = lax.all_gather(own_rows, 'dp', axis=0, tiled=True)]
    pallas_call x0 -> x1, Pallas kernels: none -> 123 us  [on_device(): pl.pallas_call(kernel, out_shape=(jax.ShapeDtypeStruct((1, 1), F32), jax....]
  transfers between devices with their start and end apart: 3 -> 0, of which waited for: 3 -> 0; matrix products, arithmetic and copies ran while one was open for 1% -> 0% of each run, Pallas kernels for 0% -> 0%
where the time goes in v1:
time: 131 us
  Pallas kernels  123 us (94%)
  local copies, waits for them, and re-layouts  5.26 us (4%)
  between operations  2.41 us (2%)
    pallas_call x1, Pallas kernels, on_device(): pl.pallas_call(kernel, out_shape=(jax.ShapeDtypeStruct((1, 1), F32), jax....  123 us
    unnamed x6, local copies, waits for them, and re-layouts  4.49 us

profile of v1, /device:TPU:1, one launch (start us, length us, event | category | flops | bytes accessed | tf_op | source)
XLA Modules:
  0.0 130.5 jit_solution(2292387087696532372)
XLA Ops:
  0.6 0.8 reshape.9.p_ref
  1.4 0.0 copy-start
  1.4 1.6 %copy-done = bf16[256,4096]{1,0:T(8,128)(2,1)S(1)} copy-done((bf16[256,4096]{1,0:T(8,128)(2,1)S(1)}, bf16[256,4096]{1,0:T(8,128)(2,1)}, u32[]{:S(2)}) %copy-start) | copy-done | bytes 2097176
  3.0 0.0 copy-start.1
  3.0 0.9 copy-done.1
  3.9 122.9 %shard_map.58 = (f32[1,1]{1,0:T(1,128)}, bf16[256,4096]{1,0:T(8,128)(2,1)S(1)}, f32[4,4096]{1,0:T(4,128)S(1)}) custom-call(bf16[256,4096]{1,0:T(8,128)(2,1)S(1)} %copy-done, bf16[2,16,512]{2,1,0:T(8,128)(2,1)S(1)} %reshape.9.p_ref, f32[256,256]{1,0:T(8,128)S(1)} %copy-done.1), custom_call_target="tpu_custom_call" | custom-call | tf_op jit(solution)/shard_map/pallas_call | solution.py:434
  127.5 1.3 %copy.11 = bf16[256,4096]{1,0:T(8,128)(2,1)} copy(bf16[256,4096]{1,0:T(8,128)(2,1)S(1)} %get-tuple-element.13) | data formatting | bytes 4194304
  128.8 0.6 copy.12
Async XLA Ops:
  1.4 1.6 %copy-start = (bf16[256,4096]{1,0:T(8,128)(2,1)S(1)}, bf16[256,4096]{1,0:T(8,128)(2,1)}, u32[]{:S(2)}) copy-start(bf16[256,4096]{1,0:T(8,128)(2,1)} %q_ref.1) | copy-start | bytes 6291460
  3.0 0.9 copy-start.1

commit v2 on v1

--- a/solution.py
+++ b/solution.py
@@ -38,15 +38,15 @@
 
 
 def kernel(
-    q_ref, p_ref, t_ref,
+    q_ref, p_hbm, t_hbm,
     loss_ref, qg_ref, pg_ref,
-    swap, stage, pa, xsrc, xgot, xstage, pb1, pb2, qh, pn, pall,
+    t_ref, p_raw, p_stage, p_ref, swap, stage, pa, xsrc, xgot, xstage, pb1, pb2, qh, pn, pall,
     student, sgot, colz, coly, rowx, lossb,
-    grads, gt, pgf, rs_out, rs_in, rs2_out, rs2_in, fin, outb,
+    grads, gt, pgf, rs_out, rs_got, rs2_out, rs2_in, fin, outb,
     q_sem, swap_s, swap_r, paz_s, paz_r, pay_s, pay_r, x_s, x_r,
-    b1_s, b1_r, b2_s, b2_r, ring1_s, ring1_r, ring2_s, ring2_r,
+    b1_s, b1_r, b2_s, b2_r, ring1_s, ring1_r, ring2_s, ring2_r, piece_s, piece_r,
     st_s, st_r, cz_s, cz_r, cy_s, cy_r, rx_s, rx_r, lo_s, lo_r,
-    g_s, g_r, ry_s, ry_r, rz_s, rz_r, f_s, f_r, o_s, o_r, own_sem,
+    g_s, g_r, ry_s, ry_r, rz_s, rz_r, f_s, f_r, o_s, o_r, own_sem, t_sem, p_sem,
 ):
     dp = lax.axis_index("dp")
     col = lax.axis_index("col")
@@ -59,6 +59,10 @@
     par = lax.rem(x, 2)
     other = 1 - core
     links = Links()
+    own_t = pltpu.make_async_copy(t_hbm, t_ref, t_sem)
+    own_t.start()
+    own_p = pltpu.make_async_copy(p_hbm.at[0], p_raw, p_sem)
+    own_p.start()
 
     def at(xx, yy, zz, cc):
         xx, yy, zz = lax.rem(xx + 4, 4), lax.rem(yy + 8, 8), lax.rem(zz + 8, 8)
@@ -94,6 +98,12 @@
     barrier = pltpu.get_barrier_semaphore()
     for device in peers:
         pl.semaphore_signal(barrier, inc=1, device_id=device, device_id_type=MESH)
+
+    own_p.wait()
+    raw = p_raw[...].astype(F32)
+    for block in range(8):
+        p_stage[block // 4, 4 * (block % 4) : 4 * (block % 4) + 4] = raw[:, 512 * block : 512 * block + 512]
+    p_ref[...] = p_stage[...].astype(BF16)
     pl.semaphore_wait(barrier, len(peers))
 
     links.send(p_ref.at[other], swap, swap_s, swap_r, sib)
@@ -177,24 +187,48 @@
         top, total = combine(coly[kind])
         return row_log, top + jnp.log(total)
 
-    def ring(me, view, device, send_sem, recv_sem):
-        for step in range(1, 5):
-            for way, sign in enumerate((1, -1)):
+    def ring(me, view, device, send_sem, recv_sem, chunks=2, pieces=None, arrived=None):
+        def at_step(step):
+            for c in range(chunks):
+                for way, sign in enumerate((1, -1)):
+                    if step < 5 or (2 * c) // chunks == way:
+                        yield c, way, sign
+
+        for step in range(1 if pieces is None else 2, 6):
+            for c, way, sign in at_step(step):
                 block = lax.rem(me - sign * (step - 1) + 8, 8)
-                for c in range(2):
-                    if step > 1:
-                        links.arrive(view(block, c), send_sem.at[way, step - 2, c], recv_sem.at[way, step - 2, c],
-                                     device(me - sign))
-                    if step == 4 and c != way:
-                        continue
+                if step == 2 and pieces is not None:
+                    if c == 0:
+                        pieces(way, block)
+                elif step > 1:
+                    links.arrive(view(block, c), send_sem.at[way, step - 2, c], recv_sem.at[way, step - 2, c],
+                                 device(me - sign))
+                    if arrived is not None:
+                        arrived(block)
+                if step < 4 or (step == 4 and (2 * c) // chunks == way):
                     links.send(view(block, c), view(block, c), send_sem.at[way, step - 1, c],
                                recv_sem.at[way, step - 1, c], device(me + sign))
             yield
-        block = lax.rem(me + 4, 8)
-        for way, sign in enumerate((1, -1)):
-            links.arrive(view(block, way), send_sem.at[way, 3, way], recv_sem.at[way, 3, way], device(me - sign))
-        yield
-
+
+    def ring_sum():
+        for step in range(1, 6):
+            for way, sign in enumerate((1, -1)):
+                block = lax.rem(y + sign * (5 - step) + 8, 8)
+                for c in range(2):
+                    if step == 1 and c != way:
+                        continue
+                    part = rs_out.at[block, pl.ds(2 * c, 2)]
+                    if step > 2 or (step == 2 and c == way):
+                        got = rs_got.at[way, step - 2, c]
+                        links.arrive(got, ry_s.at[way, step - 2, c], ry_r.at[way, step - 2, c], y_peer(y - sign))
+                        if step < 5:
+                            part[...] = (part[...].astype(F32) + got[...].astype(F32)).astype(BF16)
+                    if step < 5:
+                        links.send(part, rs_got.at[way, step - 1, c], ry_s.at[way, step - 1, c],
+                                   ry_r.at[way, step - 1, c], y_peer(y + sign))
+            yield
+
+    own_t.wait()
     teacher = t_ref[...]
     send_stats(0, teacher)
 
@@ -206,26 +240,40 @@
         both = xgot[i].astype(F32)
         xstage[8 * i : 8 * i + 8, :512] = both[:8]
         xstage[8 * i : 8 * i + 8, 512:] = both[8:]
-    pb1[y, z] = xstage[:, :512].astype(BF16)
-    pb2[z, y] = xstage[:, 512:].astype(BF16)
-
+    pb1[y, z] = xstage[:, :384].astype(BF16)
+    pb2[z, y] = xstage[:, 384:].astype(BF16)
+    order = [lax.rem(y + d, 8) for d in (0, 7, 1, 6, 2, 5, 3, 4)]
+    known = iter(range(8))
+
+    def send_piece(block):
+        k = next(known)
+        for way, sign in enumerate((1, -1)):
+            links.send(pb2.at[z, block], pb2.at[z, block], piece_s.at[way, k], piece_r.at[way, k], z_peer(z + sign))
+
+    def wait_pieces(way, block):
+        for k in range(8):
+            links.arrive(pb2.at[block, order[k]], piece_s.at[way, k], piece_r.at[way, k], z_peer(z - (1, -1)[way]))
+
+    fill1 = ring(z, lambda b, c: pb1.at[y, b], z_peer, b1_s, b1_r, chunks=1)
+    fill2 = ring(y, lambda b, c: pb2.at[z, b], y_peer, b2_s, b2_r, chunks=1, arrived=send_piece)
+    next(fill2)
+    next(fill1)
+    send_piece(y)
     for d in range(1, 4):
         i = lax.rem(zl + d, 4)
         links.arrive(pa.at[y, i], paz_s.at[d - 1], paz_r.at[i], zl_peer(i))
-    own_ring = ring(y, lambda b, c: pa.at[b, pl.ds(2 * c, 2)], y_peer, pay_s, pay_r)
-    next(own_ring)
-    for d in range(1, 8):
-        i = lax.rem(z + d, 8)
-        links.send(pb1.at[y, z], pb1.at[y, z], b1_s.at[d - 1], b1_r.at[z], z_peer(i))
+    own_ring = ring(y, lambda b, c: pa.at[b, c], y_peer, pay_s, pay_r, chunks=4)
+    def advance(*steps):
+        for step in steps:
+            next(step)
+
+    ring1 = ring(y, lambda b, c: pb1.at[b, pl.ds(4 * c, 4)], y_peer, ring1_s, ring1_r)
+    ring2 = ring(z, lambda b, c: pb2.at[b, pl.ds(4 * c, 4)], z_peer, ring2_s, ring2_r, pieces=wait_pieces)
+    advance(own_ring, fill2, fill1, own_ring, fill2, fill1)
     pass_stats(0)
-    next(own_ring)
-    next(own_ring)
-    for d in range(1, 8):
-        i = lax.rem(y + d, 8)
-        links.send(pb2.at[z, y], pb2.at[z, y], b2_s.at[d - 1], b2_r.at[y], y_peer(i))
-    next(own_ring)
+    advance(own_ring, fill2, fill1, own_ring, fill2, fill1)
     row_teacher, col_teacher = finish_stats(0)
-    next(own_ring)
+    advance(ring1, own_ring)
 
     @pl.loop(0, 16)
     def _(pair):
@@ -243,22 +291,13 @@
     links.send(student.at[1], sgot, st_s, st_r, sib)
     own_part = lax.dot_general(qh[mine], pn[...], NT, preferred_element_type=F32)
 
-    for d in range(1, 8):
-        i = lax.rem(z + d, 8)
-        links.arrive(pb1.at[y, i], b1_s.at[d - 1], b1_r.at[i], z_peer(i))
-    ring1 = ring(y, lambda b, c: pb1.at[b, pl.ds(4 * c, 4)], y_peer, ring1_s, ring1_r)
-    next(ring1)
-
     links.arrive(sgot, st_s, st_r, sib)
     scores = (own_part + sgot[...]) * INV_TEMP
     student[0] = scores
     send_stats(1, scores)
+    advance(ring2)
     pass_stats(1)
-    for d in range(1, 8):
-        i = lax.rem(y + d, 8)
-        links.arrive(pb2.at[z, i], b2_s.at[d - 1], b2_r.at[i], y_peer(i))
-    ring2 = ring(z, lambda b, c: pb2.at[b, pl.ds(4 * c, 4)], z_peer, ring2_s, ring2_r)
-    next(ring2)
+    advance(ring1)
     row_student, col_student = finish_stats(1)
 
     def down(row):
@@ -311,50 +350,40 @@
         both = jnp.concatenate([pgf[rows, :1024], pgf[rows, 1024:]], axis=0)
         rs_out[chip // 4, lax.rem(chip, 4)] = both.astype(BF16)
 
-    for d in range(1, 8):
-        i = lax.rem(y + d, 8)
-        links.send(rs_out.at[i], rs_in.at[y], ry_s.at[d - 1], ry_r.at[y], y_peer(i))
+    sums = ring_sum()
+    advance(sums)
 
     partner = grads.at[x, 1 - zh, core]
     links.arrive(partner, g_s.at[1], g_r.at[x, 1 - zh, core], at(x, y, z + 4, core))
     for d in range(1, 4):
         links.send(partner, partner, g_s.at[4 + d], g_r.at[x, 1 - zh, core], x_peer(x + d))
     links.send(partner, partner, g_s.at[8], g_r.at[x, 1 - zh, core], sib)
-    next(ring1)
-    next(ring2)
-    send_loss(1, zc, zc_peer, sum_loss(0, col, col_peer))
+    advance(ring1, ring2, sums)
     for d in range(1, 4):
         i = lax.rem(x + d, 4)
         block = grads.at[i, zh, core]
         links.arrive(block, g_s.at[1 + d], g_r.at[i, zh, core], x_peer(i))
         links.send(block, block, g_s.at[8 + d], g_r.at[i, zh, core], sib)
-    next(ring1)
-    next(ring2)
-    send_loss(2, y, y_peer, sum_loss(1, zc, zc_peer))
+    advance(sums, ring1, ring2)
+    send_loss(1, zc, zc_peer, sum_loss(0, col, col_peer))
+    advance(sums)
     for d in range(1, 4):
         i = lax.rem(x + d, 4)
         block = grads.at[i, 1 - zh, core]
         links.arrive(block, g_s.at[4 + d], g_r.at[i, 1 - zh, core], x_peer(i))
         links.send(block, block, g_s.at[11 + d], g_r.at[i, 1 - zh, core], sib)
-    next(ring1)
-    next(ring2)
-
-    total = None
-    for d in range(1, 8):
-        i = lax.rem(y + d, 8)
-        links.arrive(rs_in.at[i], ry_s.at[d - 1], ry_r.at[i], y_peer(i))
-    rs_in[y] = rs_out[y]
+    advance(sums)
     for i in range(4):
-        total = rs_in[0, i].astype(F32)
-        for j in range(1, 8):
-            total += rs_in[j, i].astype(F32)
+        total = rs_out[y, i].astype(F32)
+        for way in range(2):
+            total += rs_got[way, 3, i // 2, i % 2].astype(F32)
         rs2_out[i] = total.astype(BF16)
     for d in range(1, 4):
         i = lax.rem(zl + d, 4)
         links.send(rs2_out.at[i], rs2_in.at[zl], rz_s.at[d - 1], rz_r.at[zl], zl_peer(i))
     rs2_in[zl] = rs2_out[zl]
-    next(ring1)
-    next(ring2)
+    send_loss(2, y, y_peer, sum_loss(1, zc, zc_peer))
+    advance(ring1, ring2)
 
     @pl.loop(0, 32)
     def _(pair):
@@ -368,7 +397,7 @@
                 b0, b1 = pb2[zf, yy].astype(F32), pb2[zf + 1, yy].astype(F32)
             for i in range(4):
                 both = jnp.concatenate([b0[8 * i : 8 * i + 8], b1[8 * i : 8 * i + 8]], axis=0)
-                pall[i, group, rows, 512 * part : 512 * part + 512] = both.astype(BF16)
+                pall[i, group, rows, slice(0, 384) if part == 0 else slice(384, 1024)] = both.astype(BF16)
 
     for i in range(3):
         j = lax.rem(zl + i + 1, 4)
@@ -392,20 +421,19 @@
 
     lanes = pl.ds(pl.multiple_of(core * 2048 + par * 1024, 1024), 1024)
     for c in range(2):
-        cc = jnp.where(core == c, 1, 0)
-        del cc
         for part in range(2):
             sl = slice(512 * part, 512 * part + 512)
+            to = pl.ds(pl.multiple_of(core * 2048 + par * 1024 + 512 * part, 512), 512)
             acc = jnp.zeros((256, 512), F32)
             for i in range(4):
                 for h in range(2):
                     acc += lax.dot_general(grads[i, h, c], pall[i, h, :, sl], NN, preferred_element_type=F32)
             outb[c, :, sl] = (acc * INV_TEMP).astype(BF16)
-        for way in range(2):
-            rows = pl.ds(128 * way, 128)
-            links.send(outb.at[c, rows], qg_ref.at[rows, lanes], o_s.at[c, way], o_r.at[core, way],
-                       at(x + 1 - 2 * way, y, z, c))
-    links.send(outb.at[other], qg_ref.at[:, lanes], o_s.at[0, 2], o_r.at[core, 2], sib)
+            for way in range(2):
+                rows = pl.ds(128 * way, 128)
+                links.send(outb.at[c, rows, sl], qg_ref.at[rows, to], o_s.at[c, way, part], o_r.at[core, way, part],
+                           at(x + 1 - 2 * way, y, z, c))
+    links.send(outb.at[other], qg_ref.at[:, lanes], o_s.at[0, 2, 0], o_r.at[core, 2, 0], sib)
     own_out = pltpu.make_async_copy(outb.at[core], qg_ref.at[:, lanes], own_sem)
     own_out.start()
 
@@ -417,18 +445,18 @@
             pg_ref[:, start : start + 1024] = fin[h, 4 * k : 4 * k + 4]
 
     far = pl.ds(pl.multiple_of(other * 2048 + par * 1024, 1024), 1024)
-    links.arrive(qg_ref.at[:, far], o_s.at[0, 2], o_r.at[other, 2], sib)
+    links.arrive(qg_ref.at[:, far], o_s.at[0, 2, 0], o_r.at[other, 2, 0], sib)
     for c in range(2):
-        lanes = pl.ds(pl.multiple_of(c * 2048 + (1 - par) * 1024, 1024), 1024)
-        for way in range(2):
-            links.arrive(qg_ref.at[pl.ds(128 * way, 128), lanes], o_s.at[c, way], o_r.at[c, way],
-                         at(x - 1 + 2 * way, y, z, c))
+        for part in range(2):
+            lanes = pl.ds(pl.multiple_of(c * 2048 + (1 - par) * 1024 + 512 * part, 512), 512)
+            for way in range(2):
+                links.arrive(qg_ref.at[pl.ds(128 * way, 128), lanes], o_s.at[c, way, part], o_r.at[c, way, part],
+                             at(x - 1 + 2 * way, y, z, c))
     own_out.wait()
     links.drain()
 
 
 def on_device(queries, passages, teacher):
-    pieces = passages[0].reshape(4, 2, 4, 512).transpose(1, 2, 0, 3).reshape(2, 16, 512)
     dma = pltpu.SemaphoreType.DMA
     vmem = pltpu.VMEM
     loss, query_grads, passage_grads = pl.pallas_call(
@@ -439,24 +467,28 @@
             jax.ShapeDtypeStruct((4, 4096), F32),
         ),
         in_specs=[
-            pl.BlockSpec(memory_space=pl.ANY),
-            pl.BlockSpec(memory_space=pltpu.VMEM),
-            pl.BlockSpec(memory_space=pltpu.VMEM),
+            pl.BlockSpec(memory_space=pltpu.HBM),
+            pl.BlockSpec(memory_space=pltpu.HBM),
+            pl.BlockSpec(memory_space=pltpu.HBM),
         ],
         out_specs=(
             pl.BlockSpec(memory_space=pltpu.SMEM),
-            pl.BlockSpec(memory_space=pl.ANY),
+            pl.BlockSpec(memory_space=pltpu.HBM),
             pl.BlockSpec(memory_space=pltpu.VMEM),
         ),
         scratch_shapes=[
+            vmem((256, 256), F32),
+            vmem((4, 4096), BF16),
+            vmem((2, 16, 512), F32),
+            vmem((2, 16, 512), BF16),
             vmem((16, 512), BF16),
             vmem((16, 1024), F32),
             vmem((8, 4, 16, 1024), BF16),
             vmem((2, 16, 512), BF16),
             vmem((4, 16, 512), BF16),
             vmem((32, 1024), F32),
-            vmem((8, 8, 32, 512), BF16),
-            vmem((8, 8, 32, 512), BF16),
+            vmem((8, 8, 32, 384), BF16),
+            vmem((8, 8, 32, 640), BF16),
             vmem((512, 2048), BF16),
             vmem((256, 2048), BF16),
             vmem((4, 2, 256, 1024), BF16),
@@ -470,7 +502,7 @@
             vmem((256, 512), BF16),
             vmem((256, 2048), F32),
             vmem((8, 4, 16, 1024), BF16),
-            vmem((8, 4, 16, 1024), BF16),
+            vmem((2, 4, 2, 2, 16, 1024), BF16),
             vmem((4, 16, 1024), BF16),
             vmem((4, 16, 1024), BF16),
             vmem((2, 8, 1024), F32),
@@ -478,28 +510,29 @@
             dma((2,)),
             dma, dma,
             dma((3,)), dma((4,)),
-            dma((2, 4, 2)), dma((2, 4, 2)),
+            dma((2, 4, 4)), dma((2, 4, 4)),
             dma((3,)), dma((4,)),
-            dma((7,)), dma((8,)),
-            dma((7,)), dma((8,)),
+            dma((2, 4, 1)), dma((2, 4, 1)),
+            dma((2, 4, 1)), dma((2, 4, 1)),
             dma((2, 4, 2)), dma((2, 4, 2)),
             dma((2, 4, 2)), dma((2, 4, 2)),
+            dma((2, 8)), dma((2, 8)),
             dma, dma,
             dma((2, 7)), dma((2, 8)),
             dma((2, 7)), dma((2, 8)),
             dma((2, 7)), dma((2, 8)),
             dma((3, 7)), dma((3, 8)),
             dma((15,)), dma((4, 2, 2)),
-            dma((7,)), dma((8,)),
+            dma((2, 4, 2)), dma((2, 4, 2)),
             dma((3,)), dma((4,)),
             dma, dma,
-            dma((2, 3)), dma((2, 3)),
-            dma,
+            dma((2, 3, 2)), dma((2, 3, 2)),
+            dma, dma, dma,
         ],
         compiler_params=pltpu.CompilerParams(
-            collective_id=0, has_side_effects=True, vmem_limit_bytes=48 * 2**20
+            collective_id=0, has_side_effects=True, vmem_limit_bytes=54 * 2**20
         ),
-    )(queries, pieces, teacher)
+    )(queries, passages, teacher)
     return loss[0, 0], query_grads, passage_grads[None]
 
 

time: 131 us -> 109 us (0.83)
  Pallas kernels: 123 us -> 103 us
  local copies, waits for them, and re-layouts: 5.26 us -> 3.79 us
    pallas_call x1, Pallas kernels: 123 us -> 103 us  [on_device(): pl.pallas_call(kernel, out_shape=(jax.ShapeDtypeStruct((1, 1), F32), jax....]
    unnamed x6 -> x4, local copies, waits for them, and re-layouts: 4.49 us -> 3.79 us
where the time goes in v2:
time: 109 us
  Pallas kernels  103 us (94%)
  local copies, waits for them, and re-layouts  3.79 us (3%)
  between operations  2.34 us (2%)
    pallas_call x1, Pallas kernels, on_device(): pl.pallas_call(kernel, out_shape=(jax.ShapeDtypeStruct((1, 1), F32), jax....  103 us
    unnamed x4, local copies, waits for them, and re-layouts  3.79 us

profile of v2, /device:TPU:1, one launch (start us, length us, event | category | flops | bytes accessed | tf_op | source)
XLA Modules:
  0.0 109.1 jit_solution(15018086002293002493)
XLA Ops:
  0.6 103.0 %shard_map.58 = (f32[1,1]{1,0:T(1,128)}, bf16[256,4096]{1,0:T(8,128)(2,1)}, f32[4,4096]{1,0:T(4,128)}) custom-call(bf16[256,4096]{1,0:T(8,128)(2,1)} %q_ref.1, bf16[1,4,4096]{2,1,0:T(4,128)(2,1)} %p_hbm.1, f32[256,256]{1,0:T(8,128)} %t_hbm.1), custom_call_target="tpu_custom_call" | custom-call | tf_op jit(solution)/shard_map/pallas_call | solution.py:462
  104.2 0.0 copy-start
  104.2 3.2 %copy.10 = bf16[256,4096]{1,0:T(8,128)(2,1)} copy(bf16[256,4096]{1,0:T(8,128)(2,1)} %get-tuple-element.13) | data formatting | bytes 4194304
  107.4 0.0 copy-done
  107.4 0.6 copy.11
Async XLA Ops:
  104.2 3.2 %copy-start = (f32[4,4096]{1,0:T(4,128)S(1)}, f32[4,4096]{1,0:T(4,128)}, u32[]{:S(2)}) copy-start(f32[4,4096]{1,0:T(4,128)} %get-tuple-element.8) | copy-start | bytes 196612

commit v3 on v2

--- a/solution.py
+++ b/solution.py
@@ -145,7 +145,6 @@
         top = jnp.max(values, axis=0, keepdims=True)
         return top, jnp.sum(jnp.exp(values - top), axis=0, keepdims=True)
 
-    zeros6 = jnp.zeros((6, 256), F32)
     lane = lax.broadcasted_iota(jnp.int32, (256, 128), 1)
 
     def combine(slots):
@@ -155,13 +154,13 @@
 
     def send_stats(kind, values):
         top, total = reduce_cols(values)
-        colz[kind, zc] = jnp.concatenate([top, total, zeros6], axis=0)
+        colz[kind, zc] = jnp.concatenate([top, total], axis=0)
         for d in range(1, 8):
             links.send(colz.at[kind, zc], colz.at[kind, zc], cz_s.at[kind, d - 1], cz_r.at[kind, zc],
                        zc_peer(lax.rem(zc + d, 8)))
         top, total = reduce_rows(values)
         packed = jnp.where(lane == 0, top, jnp.where(lane == 1, total, 0.0))
-        rowx[kind, col] = packed.T[:8]
+        rowx[kind, col] = packed.T[:2]
         for d in range(1, 8):
             links.send(rowx.at[kind, col], rowx.at[kind, col], rx_s.at[kind, d - 1], rx_r.at[kind, col],
                        col_peer(lax.rem(col + d, 8)))
@@ -171,7 +170,7 @@
             i = lax.rem(zc + d, 8)
             links.arrive(colz.at[kind, i], cz_s.at[kind, d - 1], cz_r.at[kind, i], zc_peer(i))
         top, total = combine(colz[kind])
-        coly[kind, y] = jnp.concatenate([top, total, zeros6], axis=0)
+        coly[kind, y] = jnp.concatenate([top, total], axis=0)
         for d in range(1, 8):
             links.send(coly.at[kind, y], coly.at[kind, y], cy_s.at[kind, d - 1], cy_r.at[kind, y], y_peer(y + d))
 
@@ -187,7 +186,7 @@
         top, total = combine(coly[kind])
         return row_log, top + jnp.log(total)
 
-    def ring(me, view, device, send_sem, recv_sem, chunks=2, pieces=None, arrived=None):
+    def ring(me, view, device, send_sem, recv_sem, chunks=2, pieces=None, arrived=None, ready=None):
         def at_step(step):
             for c in range(chunks):
                 for way, sign in enumerate((1, -1)):
@@ -197,6 +196,8 @@
         for step in range(1 if pieces is None else 2, 6):
             for c, way, sign in at_step(step):
                 block = lax.rem(me - sign * (step - 1) + 8, 8)
+                if step == 1 and ready is not None and way == 0:
+                    ready(c)
                 if step == 2 and pieces is not None:
                     if c == 0:
                         pieces(way, block)
@@ -208,6 +209,8 @@
                 if step < 4 or (step == 4 and (2 * c) // chunks == way):
                     links.send(view(block, c), view(block, c), send_sem.at[way, step - 1, c],
                                recv_sem.at[way, step - 1, c], device(me + sign))
+                if step == 1 and ready is not None and way == 1 and c == 0:
+                    yield
             yield
 
     def ring_sum():
@@ -228,6 +231,13 @@
                                    ry_r.at[way, step - 1, c], y_peer(y + sign))
             yield
 
+    def wait_share(c):
+        if c:
+            i = lax.rem(zl + c, 4)
+            links.arrive(pa.at[y, i], paz_s.at[c - 1], paz_r.at[i], zl_peer(i))
+
+    own_ring = ring(y, lambda b, c: pa.at[b, lax.rem(zl + c, 4)], y_peer, pay_s, pay_r, chunks=4, ready=wait_share)
+    next(own_ring)
     own_t.wait()
     teacher = t_ref[...]
     send_stats(0, teacher)
@@ -259,10 +269,6 @@
     next(fill2)
     next(fill1)
     send_piece(y)
-    for d in range(1, 4):
-        i = lax.rem(zl + d, 4)
-        links.arrive(pa.at[y, i], paz_s.at[d - 1], paz_r.at[i], zl_peer(i))
-    own_ring = ring(y, lambda b, c: pa.at[b, c], y_peer, pay_s, pay_r, chunks=4)
     def advance(*steps):
         for step in steps:
             next(step)
@@ -316,6 +322,7 @@
     for d in range(1, 4):
         links.send(own_grads, own_grads, g_s.at[1 + d], g_r.at[x, zh, core], x_peer(x + d))
 
+    advance(ring2)
     terms = (row_target + col_target) * (teacher - scores)
     terms = jnp.sum(terms.reshape(32, 8, 256), axis=0)
     once = jnp.where(col == 0, 1.0, 0.0) * (row_student - row_teacher)
@@ -351,39 +358,26 @@
         rs_out[chip // 4, lax.rem(chip, 4)] = both.astype(BF16)
 
     sums = ring_sum()
-    advance(sums)
+    advance(sums, ring1, sums)
 
     partner = grads.at[x, 1 - zh, core]
     links.arrive(partner, g_s.at[1], g_r.at[x, 1 - zh, core], at(x, y, z + 4, core))
     for d in range(1, 4):
         links.send(partner, partner, g_s.at[4 + d], g_r.at[x, 1 - zh, core], x_peer(x + d))
     links.send(partner, partner, g_s.at[8], g_r.at[x, 1 - zh, core], sib)
-    advance(ring1, ring2, sums)
     for d in range(1, 4):
         i = lax.rem(x + d, 4)
         block = grads.at[i, zh, core]
         links.arrive(block, g_s.at[1 + d], g_r.at[i, zh, core], x_peer(i))
         links.send(block, block, g_s.at[8 + d], g_r.at[i, zh, core], sib)
-    advance(sums, ring1, ring2)
-    send_loss(1, zc, zc_peer, sum_loss(0, col, col_peer))
-    advance(sums)
+    advance(ring2, ring1, sums)
     for d in range(1, 4):
         i = lax.rem(x + d, 4)
         block = grads.at[i, 1 - zh, core]
         links.arrive(block, g_s.at[4 + d], g_r.at[i, 1 - zh, core], x_peer(i))
         links.send(block, block, g_s.at[11 + d], g_r.at[i, 1 - zh, core], sib)
-    advance(sums)
-    for i in range(4):
-        total = rs_out[y, i].astype(F32)
-        for way in range(2):
-            total += rs_got[way, 3, i // 2, i % 2].astype(F32)
-        rs2_out[i] = total.astype(BF16)
-    for d in range(1, 4):
-        i = lax.rem(zl + d, 4)
-        links.send(rs2_out.at[i], rs2_in.at[zl], rz_s.at[d - 1], rz_r.at[zl], zl_peer(i))
-    rs2_in[zl] = rs2_out[zl]
-    send_loss(2, y, y_peer, sum_loss(1, zc, zc_peer))
-    advance(ring1, ring2)
+    advance(sums, ring1, ring2)
+    send_loss(1, zc, zc_peer, sum_loss(0, col, col_peer))
 
     @pl.loop(0, 32)
     def _(pair):
@@ -398,18 +392,6 @@
             for i in range(4):
                 both = jnp.concatenate([b0[8 * i : 8 * i + 8], b1[8 * i : 8 * i + 8]], axis=0)
                 pall[i, group, rows, slice(0, 384) if part == 0 else slice(384, 1024)] = both.astype(BF16)
-
-    for i in range(3):
-        j = lax.rem(zl + i + 1, 4)
-        links.arrive(rs2_in.at[j], rz_s.at[i], rz_r.at[j], zl_peer(j))
-    total = rs2_in[0].astype(F32)
-    for j in range(1, 4):
-        total += rs2_in[j].astype(F32)
-    for c in range(2):
-        piece = jnp.concatenate([total[4 * c : 4 * c + 4], total[8 + 4 * c : 12 + 4 * c]], axis=0)
-        stage[8 * c : 8 * c + 8] = piece
-    fin[core] = stage[pl.ds(pl.multiple_of(core * 8, 8), 8)]
-    links.send(stage.at[pl.ds(pl.multiple_of(other * 8, 8), 8)], fin.at[core], f_s, f_r, sib)
 
     for i in range(4):
         for h in range(2):
@@ -436,6 +418,30 @@
     links.send(outb.at[other], qg_ref.at[:, lanes], o_s.at[0, 2, 0], o_r.at[core, 2, 0], sib)
     own_out = pltpu.make_async_copy(outb.at[core], qg_ref.at[:, lanes], own_sem)
     own_out.start()
+
+    send_loss(2, y, y_peer, sum_loss(1, zc, zc_peer))
+    advance(sums)
+    for i in range(4):
+        total = rs_out[y, i].astype(F32)
+        for way in range(2):
+            total += rs_got[way, 3, i // 2, i % 2].astype(F32)
+        rs2_out[i] = total.astype(BF16)
+    for d in range(1, 4):
+        i = lax.rem(zl + d, 4)
+        links.send(rs2_out.at[i], rs2_in.at[zl], rz_s.at[d - 1], rz_r.at[zl], zl_peer(i))
+    rs2_in[zl] = rs2_out[zl]
+    for i in range(3):
+        j = lax.rem(zl + i + 1, 4)
+        links.arrive(rs2_in.at[j], rz_s.at[i], rz_r.at[j], zl_peer(j))
+    total = rs2_in[0].astype(F32)
+    for j in range(1, 4):
+        total += rs2_in[j].astype(F32)
+    for c in range(2):
+        piece = jnp.concatenate([total[4 * c : 4 * c + 4], total[8 + 4 * c : 12 + 4 * c]], axis=0)
+        stage[8 * c : 8 * c + 8] = piece
+    fin[core] = stage[pl.ds(pl.multiple_of(core * 8, 8), 8)]
+    links.send(stage.at[pl.ds(pl.multiple_of(other * 8, 8), 8)], fin.at[core], f_s, f_r, sib)
+
 
     loss_ref[0, 0] = jnp.sum(sum_loss(2, y, y_peer)) / (256 * 64 + 256 * 8)
     links.arrive(fin.at[other], f_s, f_r, sib)
@@ -494,9 +500,9 @@
             vmem((4, 2, 256, 1024), BF16),
             vmem((2, 256, 256), F32),
             vmem((256, 256), F32),
-            vmem((2, 8, 8, 256), F32),
-            vmem((2, 8, 8, 256), F32),
-            vmem((2, 8, 8, 256), F32),
+            vmem((2, 8, 2, 256), F32),
+            vmem((2, 8, 2, 256), F32),
+            vmem((2, 8, 2, 256), F32),
             vmem((3, 8, 8, 128), F32),
             vmem((4, 2, 2, 256, 256), BF16),
             vmem((256, 512), BF16),

time: 109 us -> 97.7 us (0.90)
  Pallas kernels: 103 us -> 91.4 us
    pallas_call x1, Pallas kernels: 103 us -> 91.4 us  [on_device(): pl.pallas_call(kernel, out_shape=(jax.ShapeDtypeStruct((1, 1), F32), jax....]
where the time goes in v3:
time: 97.7 us; the launch traced here: 97.5 us
  Pallas kernels  91.4 us (94%)
  local copies, waits for them, and re-layouts  3.79 us (4%)
  between operations  2.34 us (2%)
    pallas_call x1, Pallas kernels, on_device(): pl.pallas_call(kernel, out_shape=(jax.ShapeDtypeStruct((1, 1), F32), jax....  91.4 us
    unnamed x4, local copies, waits for them, and re-layouts  3.79 us

profile of v3, /device:TPU:1, one launch (start us, length us, event | category | flops | bytes accessed | tf_op | source)
XLA Modules:
  0.0 97.5 jit_solution(15897407077657709707)
XLA Ops:
  0.6 91.4 %shard_map.58 = (f32[1,1]{1,0:T(1,128)}, bf16[256,4096]{1,0:T(8,128)(2,1)}, f32[4,4096]{1,0:T(4,128)}) custom-call(bf16[256,4096]{1,0:T(8,128)(2,1)} %q_ref.1, bf16[1,4,4096]{2,1,0:T(4,128)(2,1)} %p_hbm.1, f32[256,256]{1,0:T(8,128)} %t_hbm.1), custom_call_target="tpu_custom_call" | custom-call | tf_op jit(solution)/shard_map/pallas_call | solution.py:468
  92.6 0.0 copy-start
  92.6 3.2 %copy.10 = bf16[256,4096]{1,0:T(8,128)(2,1)} copy(bf16[256,4096]{1,0:T(8,128)(2,1)} %get-tuple-element.13) | data formatting | bytes 4194304
  95.8 0.0 copy-done
  95.8 0.6 copy.11
Async XLA Ops:
  92.6 3.2 %copy-start = (f32[4,4096]{1,0:T(4,128)S(1)}, f32[4,4096]{1,0:T(4,128)}, u32[]{:S(2)}) copy-start(f32[4,4096]{1,0:T(4,128)} %get-tuple-element.8) | copy-start | bytes 196612

commit v4 on v3

--- a/solution.py
+++ b/solution.py
@@ -9,6 +9,7 @@
 
 INV_TEMP = 50.0
 MESH = pl.DeviceIdType.MESH
+SPLIT = 128
 F32 = jnp.float32
 BF16 = jnp.bfloat16
 NT = (((1,), (1,)), ((), ()))
@@ -44,7 +45,7 @@
     student, sgot, colz, coly, rowx, lossb,
     grads, gt, pgf, rs_out, rs_got, rs2_out, rs2_in, fin, outb,
     q_sem, swap_s, swap_r, paz_s, paz_r, pay_s, pay_r, x_s, x_r,
-    b1_s, b1_r, b2_s, b2_r, ring1_s, ring1_r, ring2_s, ring2_r, piece_s, piece_r,
+    b1_s, b1_r, b2_s, b2_r, ring1_s, ring1_r, ring2_s, ring2_r, piece_s, piece_r, near_s, near_r,
     st_s, st_r, cz_s, cz_r, cy_s, cy_r, rx_s, rx_r, lo_s, lo_r,
     g_s, g_r, ry_s, ry_r, rz_s, rz_r, f_s, f_r, o_s, o_r, own_sem, t_sem, p_sem,
 ):
@@ -246,12 +247,15 @@
     for d in range(1, 4):
         i = lax.rem(x + d, 4)
         links.arrive(xgot.at[i], x_s.at[d - 1], x_r.at[i], x_peer(i))
-    for i in range(4):
-        both = xgot[i].astype(F32)
-        xstage[8 * i : 8 * i + 8, :512] = both[:8]
-        xstage[8 * i : 8 * i + 8, 512:] = both[8:]
-    pb1[y, z] = xstage[:, :384].astype(BF16)
-    pb2[z, y] = xstage[:, 384:].astype(BF16)
+    for j in range(2):
+        for first, i in ((0, 2 * j + par), (16, 2 * j + 1 - par)):
+            both = xgot[i].astype(F32)
+            row = first + 8 * j
+            xstage[row : row + 8, :512] = both[:8]
+            xstage[row : row + 8, 512:] = both[8:]
+    pb1[y, z, :, :1024] = xstage[16:].astype(BF16)
+    pb1[y, z, :, 1024:] = xstage[:16, :SPLIT].astype(BF16)
+    pb2[z, y] = xstage[:16, SPLIT:].astype(BF16)
     order = [lax.rem(y + d, 8) for d in (0, 7, 1, 6, 2, 5, 3, 4)]
     known = iter(range(8))
 
@@ -273,23 +277,48 @@
         for step in steps:
             next(step)
 
-    ring1 = ring(y, lambda b, c: pb1.at[b, pl.ds(4 * c, 4)], y_peer, ring1_s, ring1_r)
-    ring2 = ring(z, lambda b, c: pb2.at[b, pl.ds(4 * c, 4)], z_peer, ring2_s, ring2_r, pieces=wait_pieces)
-    advance(own_ring, fill2, fill1, own_ring, fill2, fill1)
+    def over_y(block, c):
+        if c % 2 == 0:
+            return pb1.at[block, pl.ds(4 * (1 - zh) + c, 2)]
+        return pb1.at[block, pl.ds(4 * zh + c - 1, 2), :, pl.ds(1024, SPLIT)]
+
+    ring1 = ring(y, over_y, y_peer, ring1_s, ring1_r, chunks=4)
+    ring2 = ring(z, lambda b, c: pb2.at[b, pl.ds(2 * c, 2)], z_peer, ring2_s, ring2_r, chunks=4,
+                 pieces=wait_pieces)
+    far_lanes = pl.ds(pl.multiple_of((1 - par) * 1024, 1024), 1024)
+    placed = iter(range(8))
+
+    def place(block):
+        for pair in range(2):
+            b0 = pa[block, 2 * pair].astype(F32)
+            b1 = pa[block, 2 * pair + 1].astype(F32)
+            rows = pl.ds(pl.multiple_of(block * 32 + 16 * pair, 16), 16)
+            for k in range(2):
+                both = jnp.concatenate([b0[8 * k : 8 * k + 8], b1[8 * k : 8 * k + 8]], axis=0)
+                pn[rows, 1024 * k : 1024 * k + 1024] = both.astype(BF16)
+        k = next(placed)
+        rows = pl.ds(pl.multiple_of(block * 32, 32), 32)
+        for way, sign in enumerate((1, -1)):
+            links.send(pn.at[rows, far_lanes], pall.at[x, zh, rows], near_s.at[way, k], near_r.at[way, k],
+                       x_peer(x + sign + 4))
+
+    advance(own_ring)
+    place(y)
+    advance(fill2, fill1, own_ring)
+    place(order[1])
+    place(order[2])
+    advance(fill2, fill1)
     pass_stats(0)
-    advance(own_ring, fill2, fill1, own_ring, fill2, fill1)
+    advance(own_ring)
+    place(order[3])
+    place(order[4])
+    advance(fill2, fill1, own_ring)
+    place(order[5])
+    place(order[6])
+    advance(fill2, fill1)
     row_teacher, col_teacher = finish_stats(0)
     advance(ring1, own_ring)
-
-    @pl.loop(0, 16)
-    def _(pair):
-        yy, zz = pair // 2, lax.rem(pair, 2) * 2
-        b0 = pa[yy, zz].astype(F32)
-        b1 = pa[yy, zz + 1].astype(F32)
-        rows = pl.ds(pl.multiple_of(pair * 16, 16), 16)
-        for k in range(2):
-            both = jnp.concatenate([b0[8 * k : 8 * k + 8], b1[8 * k : 8 * k + 8]], axis=0)
-            pn[rows, 1024 * k : 1024 * k + 1024] = both.astype(BF16)
+    place(order[7])
 
     own_q.wait()
     links.arrive(qh.at[theirs], q_sem.at[0], q_sem.at[1], sib)
@@ -358,7 +387,7 @@
         rs_out[chip // 4, lax.rem(chip, 4)] = both.astype(BF16)
 
     sums = ring_sum()
-    advance(sums, ring1, sums)
+    advance(sums, ring1, sums, ring1)
 
     partner = grads.at[x, 1 - zh, core]
     links.arrive(partner, g_s.at[1], g_r.at[x, 1 - zh, core], at(x, y, z + 4, core))
@@ -370,29 +399,41 @@
         block = grads.at[i, zh, core]
         links.arrive(block, g_s.at[1 + d], g_r.at[i, zh, core], x_peer(i))
         links.send(block, block, g_s.at[8 + d], g_r.at[i, zh, core], sib)
-    advance(ring2, ring1, sums)
+    advance(ring2, sums)
     for d in range(1, 4):
         i = lax.rem(x + d, 4)
         block = grads.at[i, 1 - zh, core]
         links.arrive(block, g_s.at[4 + d], g_r.at[i, 1 - zh, core], x_peer(i))
         links.send(block, block, g_s.at[11 + d], g_r.at[i, 1 - zh, core], sib)
-    advance(sums, ring1, ring2)
+    advance(ring1, sums, ring2)
     send_loss(1, zc, zc_peer, sum_loss(0, col, col_peer))
 
     @pl.loop(0, 32)
     def _(pair):
         group, yy, zz = pair // 16, lax.rem(pair // 2, 8), lax.rem(pair, 2) * 2
         rows = pl.ds(pl.multiple_of(lax.rem(pair, 16) * 16, 16), 16)
-        for part in range(2):
-            zf = group * 4 + zz
-            if part == 0:
-                b0, b1 = pb1[yy, zf].astype(F32), pb1[yy, zf + 1].astype(F32)
-            else:
-                b0, b1 = pb2[zf, yy].astype(F32), pb2[zf + 1, yy].astype(F32)
-            for i in range(4):
-                both = jnp.concatenate([b0[8 * i : 8 * i + 8], b1[8 * i : 8 * i + 8]], axis=0)
-                pall[i, group, rows, slice(0, 384) if part == 0 else slice(384, 1024)] = both.astype(BF16)
-
+        zf = group * 4 + zz
+        b0, b1 = pb1[yy, zf, :, 1024:].astype(F32), pb1[yy, zf + 1, :, 1024:].astype(F32)
+        c0, c1 = pb2[zf, yy].astype(F32), pb2[zf + 1, yy].astype(F32)
+        for j in range(2):
+            r = slice(8 * j, 8 * j + 8)
+            pall[2 * j + par, group, rows, :SPLIT] = jnp.concatenate([b0[r], b1[r]], axis=0).astype(BF16)
+            pall[2 * j + par, group, rows, SPLIT:] = jnp.concatenate([c0[r], c1[r]], axis=0).astype(BF16)
+
+    @pl.loop(0, 16)
+    def _(pair):
+        yy, zf = pair // 2, 4 * (1 - zh) + lax.rem(pair, 2) * 2
+        rows = pl.ds(pl.multiple_of(pair * 16, 16), 16)
+        b0, b1 = pb1[yy, zf, :, :1024].astype(F32), pb1[yy, zf + 1, :, :1024].astype(F32)
+        for j in range(2):
+            r = slice(8 * j, 8 * j + 8)
+            pall[2 * j + 1 - par, 1 - zh, rows] = jnp.concatenate([b0[r], b1[r]], axis=0).astype(BF16)
+
+    for way, sign in enumerate((1, -1)):
+        i = lax.rem(x - sign + 4, 4)
+        for k in range(8):
+            rows = pl.ds(pl.multiple_of(order[k] * 32, 32), 32)
+            links.arrive(pall.at[i, zh, rows], near_s.at[way, k], near_r.at[way, k], x_peer(i))
     for i in range(4):
         for h in range(2):
             i_dyn = lax.rem(x + i, 4)
@@ -419,7 +460,6 @@
     own_out = pltpu.make_async_copy(outb.at[core], qg_ref.at[:, lanes], own_sem)
     own_out.start()
 
-    send_loss(2, y, y_peer, sum_loss(1, zc, zc_peer))
     advance(sums)
     for i in range(4):
         total = rs_out[y, i].astype(F32)
@@ -430,6 +470,7 @@
         i = lax.rem(zl + d, 4)
         links.send(rs2_out.at[i], rs2_in.at[zl], rz_s.at[d - 1], rz_r.at[zl], zl_peer(i))
     rs2_in[zl] = rs2_out[zl]
+    send_loss(2, y, y_peer, sum_loss(1, zc, zc_peer))
     for i in range(3):
         j = lax.rem(zl + i + 1, 4)
         links.arrive(rs2_in.at[j], rz_s.at[i], rz_r.at[j], zl_peer(j))
@@ -493,8 +534,8 @@
             vmem((2, 16, 512), BF16),
             vmem((4, 16, 512), BF16),
             vmem((32, 1024), F32),
-            vmem((8, 8, 32, 384), BF16),
-            vmem((8, 8, 32, 640), BF16),
+            vmem((8, 8, 16, 1024 + SPLIT), BF16),
+            vmem((8, 8, 16, 1024 - SPLIT), BF16),
             vmem((512, 2048), BF16),
             vmem((256, 2048), BF16),
             vmem((4, 2, 256, 1024), BF16),
@@ -520,8 +561,9 @@
             dma((3,)), dma((4,)),
             dma((2, 4, 1)), dma((2, 4, 1)),
             dma((2, 4, 1)), dma((2, 4, 1)),
-            dma((2, 4, 2)), dma((2, 4, 2)),
-            dma((2, 4, 2)), dma((2, 4, 2)),
+            dma((2, 4, 4)), dma((2, 4, 4)),
+            dma((2, 4, 4)), dma((2, 4, 4)),
+            dma((2, 8)), dma((2, 8)),
             dma((2, 8)), dma((2, 8)),
             dma, dma,
             dma((2, 7)), dma((2, 8)),

time: 97.7 us -> 95.3 us (0.975)
  Pallas kernels: 91.4 us -> 89 us
    pallas_call x1, Pallas kernels: 91.4 us -> 89 us  [on_device(): pl.pallas_call(kernel, out_shape=(jax.ShapeDtypeStruct((1, 1), F32), jax....]
where the time goes in v4:
time: 95.3 us; the launch traced here: 95.1 us
  Pallas kernels  89 us (93%)
  local copies, waits for them, and re-layouts  3.79 us (4%)
  between operations  2.34 us (2%)
    pallas_call x1, Pallas kernels, on_device(): pl.pallas_call(kernel, out_shape=(jax.ShapeDtypeStruct((1, 1), F32), jax....  89 us
    unnamed x4, local copies, waits for them, and re-layouts  3.79 us

profile of v4, /device:TPU:1, one launch (start us, length us, event | category | flops | bytes accessed | tf_op | source)
XLA Modules:
  0.0 95.1 jit_solution(5904483165690319104)
XLA Ops:
  0.6 89.0 %shard_map.58 = (f32[1,1]{1,0:T(1,128)}, bf16[256,4096]{1,0:T(8,128)(2,1)}, f32[4,4096]{1,0:T(4,128)}) custom-call(bf16[256,4096]{1,0:T(8,128)(2,1)} %q_ref.1, bf16[1,4,4096]{2,1,0:T(4,128)(2,1)} %p_hbm.1, f32[256,256]{1,0:T(8,128)} %t_hbm.1), custom_call_target="tpu_custom_call" | custom-call | tf_op jit(solution)/shard_map/pallas_call | solution.py:509
  90.2 0.0 copy-start
  90.2 3.2 %copy.10 = bf16[256,4096]{1,0:T(8,128)(2,1)} copy(bf16[256,4096]{1,0:T(8,128)(2,1)} %get-tuple-element.13) | data formatting | bytes 4194304
  93.3 0.0 copy-done
  93.3 0.6 copy.11
Async XLA Ops:
  90.2 3.2 %copy-start = (f32[4,4096]{1,0:T(4,128)S(1)}, f32[4,4096]{1,0:T(4,128)}, u32[]{:S(2)}) copy-start(f32[4,4096]{1,0:T(4,128)} %get-tuple-element.8) | copy-start | bytes 196612

commit v5 on v4

--- a/solution.py
+++ b/solution.py
@@ -47,7 +47,7 @@
     q_sem, swap_s, swap_r, paz_s, paz_r, pay_s, pay_r, x_s, x_r,
     b1_s, b1_r, b2_s, b2_r, ring1_s, ring1_r, ring2_s, ring2_r, piece_s, piece_r, near_s, near_r,
     st_s, st_r, cz_s, cz_r, cy_s, cy_r, rx_s, rx_r, lo_s, lo_r,
-    g_s, g_r, ry_s, ry_r, rz_s, rz_r, f_s, f_r, o_s, o_r, own_sem, t_sem, p_sem,
+    g_s, g_r, gp_s, gp_r, gx_s, gx_r, ry_s, ry_r, rz_s, rz_r, f_s, f_r, o_s, o_r, own_sem, t_sem, p_sem,
 ):
     dp = lax.axis_index("dp")
     col = lax.axis_index("col")
@@ -347,7 +347,10 @@
 
     own_grads = grads.at[x, zh, core]
     links.send(own_grads, own_grads, g_s.at[0], g_r.at[x, zh, core], sib)
-    links.send(own_grads, own_grads, g_s.at[1], g_r.at[x, zh, core], at(x, y, z + 4, core))
+    halves = [pl.ds(0, 128), pl.ds(128, 128)]
+    for c, rows in enumerate(halves):
+        part = grads.at[x, zh, core, rows]
+        links.send(part, part, gp_s.at[c], gp_r.at[c], at(x, y, z + 4, core))
     for d in range(1, 4):
         links.send(own_grads, own_grads, g_s.at[1 + d], g_r.at[x, zh, core], x_peer(x + d))
 
@@ -387,12 +390,16 @@
         rs_out[chip // 4, lax.rem(chip, 4)] = both.astype(BF16)
 
     sums = ring_sum()
-    advance(sums, ring1, sums, ring1)
+    advance(sums, ring1, sums)
 
     partner = grads.at[x, 1 - zh, core]
-    links.arrive(partner, g_s.at[1], g_r.at[x, 1 - zh, core], at(x, y, z + 4, core))
-    for d in range(1, 4):
-        links.send(partner, partner, g_s.at[4 + d], g_r.at[x, 1 - zh, core], x_peer(x + d))
+    for c, rows in enumerate(halves):
+        part = grads.at[x, 1 - zh, core, rows]
+        links.arrive(part, gp_s.at[c], gp_r.at[c], at(x, y, z + 4, core))
+        for d in range(1, 4):
+            links.send(part, part, gx_s.at[d - 1, c], gx_r.at[x, c], x_peer(x + d))
+        if c == 0:
+            advance(ring1)
     links.send(partner, partner, g_s.at[8], g_r.at[x, 1 - zh, core], sib)
     for d in range(1, 4):
         i = lax.rem(x + d, 4)
@@ -403,9 +410,10 @@
     for d in range(1, 4):
         i = lax.rem(x + d, 4)
         block = grads.at[i, 1 - zh, core]
-        links.arrive(block, g_s.at[4 + d], g_r.at[i, 1 - zh, core], x_peer(i))
+        for c, rows in enumerate(halves):
+            links.arrive(grads.at[i, 1 - zh, core, rows], gx_s.at[d - 1, c], gx_r.at[i, c], x_peer(i))
         links.send(block, block, g_s.at[11 + d], g_r.at[i, 1 - zh, core], sib)
-    advance(ring1, sums, ring2)
+    advance(ring1, ring2)
     send_loss(1, zc, zc_peer, sum_loss(0, col, col_peer))
 
     @pl.loop(0, 32)
@@ -456,6 +464,8 @@
                 rows = pl.ds(128 * way, 128)
                 links.send(outb.at[c, rows, sl], qg_ref.at[rows, to], o_s.at[c, way, part], o_r.at[core, way, part],
                            at(x + 1 - 2 * way, y, z, c))
+        if c == 0:
+            advance(sums)
     links.send(outb.at[other], qg_ref.at[:, lanes], o_s.at[0, 2, 0], o_r.at[core, 2, 0], sib)
     own_out = pltpu.make_async_copy(outb.at[core], qg_ref.at[:, lanes], own_sem)
     own_out.start()
@@ -571,6 +581,7 @@
             dma((2, 7)), dma((2, 8)),
             dma((3, 7)), dma((3, 8)),
             dma((15,)), dma((4, 2, 2)),
+            dma((2,)), dma((2,)), dma((3, 2)), dma((4, 2)),
             dma((2, 4, 2)), dma((2, 4, 2)),
             dma((3,)), dma((4,)),
             dma, dma,

time: 95.3 us -> 92.6 us (0.972)
  Pallas kernels: 89 us -> 86.3 us
    pallas_call x1, Pallas kernels: 89 us -> 86.3 us  [on_device(): pl.pallas_call(kernel, out_shape=(jax.ShapeDtypeStruct((1, 1), F32), jax....]
where the time goes in v5:
time: 92.6 us; the launch traced here: 92.5 us
  Pallas kernels  86.3 us (93%)
  local copies, waits for them, and re-layouts  3.79 us (4%)
  between operations  2.34 us (3%)
    pallas_call x1, Pallas kernels, on_device(): pl.pallas_call(kernel, out_shape=(jax.ShapeDtypeStruct((1, 1), F32), jax....  86.3 us
    unnamed x4, local copies, waits for them, and re-layouts  3.79 us

profile of v5, /device:TPU:1, one launch (start us, length us, event | category | flops | bytes accessed | tf_op | source)
XLA Modules:
  0.0 92.5 jit_solution(9478342018875334170)
XLA Ops:
  0.6 86.3 %shard_map.58 = (f32[1,1]{1,0:T(1,128)}, bf16[256,4096]{1,0:T(8,128)(2,1)}, f32[4,4096]{1,0:T(4,128)}) custom-call(bf16[256,4096]{1,0:T(8,128)(2,1)} %q_ref.1, bf16[1,4,4096]{2,1,0:T(4,128)(2,1)} %p_hbm.1, f32[256,256]{1,0:T(8,128)} %t_hbm.1), custom_call_target="tpu_custom_call" | custom-call | tf_op jit(solution)/shard_map/pallas_call | solution.py:519
  87.5 0.0 copy-start
  87.5 3.2 %copy.10 = bf16[256,4096]{1,0:T(8,128)(2,1)} copy(bf16[256,4096]{1,0:T(8,128)(2,1)} %get-tuple-element.13) | data formatting | bytes 4194304
  90.7 0.0 copy-done
  90.7 0.6 copy.11
Async XLA Ops:
  87.5 3.2 %copy-start = (f32[4,4096]{1,0:T(4,128)S(1)}, f32[4,4096]{1,0:T(4,128)}, u32[]{:S(2)}) copy-start(f32[4,4096]{1,0:T(4,128)} %get-tuple-element.8) | copy-start | bytes 196612
